TPU v7x, 32 devices: a whole 2x2x4 slice. The times are simulated.
32 devices in a mesh: dp: 4 (over y, x), expert: 8 (over z, core).
Axes of the slice: x: 2, y: 2, z: 4, core: 2. Of those that a mesh axis runs over, the one named last changes fastest.
Arguments:
- tokens: bfloat16 [1024, 6144], P('expert', 'dp'), may hold values from -6 to 6
- expert_ids: int32 [1024, 4], P('expert'), may hold values from 0 to 7, all different within a row; in each aligned block of 128 rows (0 to 127, 128 to 255, ...) at most 96 rows name the same one
- route_weights: float32 [1024, 4], P('expert'), may hold values from 0.2 to 1
- gate_weights: bfloat16 [8, 6144, 2048], P('expert', None, 'dp'), may hold values from -0.078125 to 0.078125
- up_weights: bfloat16 [8, 6144, 2048], P('expert', None, 'dp'), may hold values from -0.078125 to 0.078125
- down_weights: bfloat16 [8, 2048, 6144], P('expert', 'dp'), may hold values from -0.125 to 0.125
- grad_out: bfloat16 [1024, 6144], P('expert', 'dp'), may hold values from -6 to 6
Outputs:
- mixed: bfloat16 [1024, 6144], P('expert', 'dp')
- token_grad: bfloat16 [1024, 6144], P('expert', 'dp')
- route_grad: float32 [1024, 4], P('expert')
- gate_grad: bfloat16 [8, 6144, 2048], P('expert', None, 'dp')
- up_grad: bfloat16 [8, 6144, 2048], P('expert', None, 'dp')
- down_grad: bfloat16 [8, 2048, 6144], P('expert', 'dp')
Inputs may be any that keep to these rules, and one draw needn't show every extreme that they name: `expert_ids`: the 4 experts of a token differ; in every block of 128 consecutive tokens (the tokens of one index of the expert axis) no expert is chosen by more than 96 tokens, and some expert is chosen by exactly 96 in some blocks.
All inputs are finite; a program needn't handle non-finite values.
Results may differ from a plain program's by a relative error of at most 0.014.
Values may be sent and summed in bfloat16 or wider, within the bound.
A program may use at most 192 MiB of HBM per device.

v0:
```python
import jax
import jax.numpy as jnp
from jax import lax
from jax.sharding import PartitionSpec as P

contract_last = (((1,), (1,)), ((), ()))
contract_first = (((0,), (0,)), ((), ()))


def full_rows(block):
    return lax.all_gather(block, "dp", axis=1, tiled=True)


def dispatch(blocks):
    return lax.all_to_all(blocks, "expert", split_axis=0, concat_axis=0, tiled=True)


def send_back(blocks):
    return lax.all_to_all(blocks, "expert", split_axis=0, concat_axis=0, tiled=True)


def share_sum(partial_value):
    return lax.psum_scatter(partial_value, "dp", scatter_dimension=1, tiled=True).astype(
        jnp.float32
    )


def shards(tokens, expert_ids, route_weights, gate_weights, up_weights, down_weights, grad_out):
    expert_count = lax.axis_size("expert")
    token_count = tokens.shape[0]
    top_count = expert_ids.shape[1]
    slot_count = min(token_count, 3 * token_count * top_count // (2 * expert_count))
    assigned = token_count * top_count
    local_rows = expert_count * slot_count
    gate_weight = gate_weights[0]
    up_weight = up_weights[0]
    down_weight = down_weights[0]
    flat_ids = expert_ids.reshape(assigned)
    choose = (flat_ids[:, None] == jnp.arange(expert_count, dtype=jnp.int32)[None, :]).astype(
        jnp.int32
    )
    earlier = jnp.cumsum(choose, axis=0) - choose
    rank_in_slot = jnp.sum(earlier * choose, axis=1)
    positions = flat_ids * slot_count + rank_in_slot
    placement = (jnp.arange(local_rows, dtype=jnp.int32)[:, None] == positions[None, :]).astype(
        jnp.bfloat16
    )
    by_token = jnp.sum(placement.reshape(local_rows, token_count, top_count), axis=2)
    whole = full_rows(tokens)
    send_tokens = jnp.dot(by_token, whole, preferred_element_type=jnp.float32).astype(jnp.bfloat16)
    recv_tokens = dispatch(send_tokens.reshape(expert_count, slot_count, whole.shape[1]))
    features = recv_tokens.shape[2]
    recv_tokens = recv_tokens.reshape(local_rows, features)
    gate_pre = jnp.dot(recv_tokens, gate_weight, preferred_element_type=jnp.float32)
    up_pre = jnp.dot(recv_tokens, up_weight, preferred_element_type=jnp.float32)
    gate_sigmoid = jax.nn.sigmoid(gate_pre)
    hidden = (gate_pre * gate_sigmoid * up_pre).astype(jnp.bfloat16)
    down_part = jnp.dot(hidden, down_weight, preferred_element_type=jnp.float32).astype(
        jnp.bfloat16
    )
    expert_out = share_sum(down_part).astype(jnp.bfloat16)
    slice_width = expert_out.shape[1]
    back_out = send_back(expert_out.reshape(expert_count, slot_count, slice_width)).reshape(
        local_rows, slice_width
    )
    slot_out = lax.dot_general(
        placement, back_out, contract_first, preferred_element_type=jnp.float32
    )
    slot_out = slot_out.reshape(token_count, top_count, slice_width)
    mixed = jnp.sum(route_weights[:, :, None] * slot_out, axis=1).astype(jnp.bfloat16)
    route_part = jnp.sum(slot_out * grad_out[:, None, :].astype(jnp.float32), axis=2)
    route_grad = lax.psum(route_part, "dp")
    whole_grad = full_rows(grad_out)
    scaled = (route_weights[:, :, None] * whole_grad[:, None, :].astype(jnp.float32)).astype(
        jnp.bfloat16
    )
    send_grads = jnp.dot(
        placement, scaled.reshape(assigned, features), preferred_element_type=jnp.float32
    ).astype(jnp.bfloat16)
    recv_grads = dispatch(send_grads.reshape(expert_count, slot_count, features))
    recv_grads = recv_grads.reshape(local_rows, features)
    hidden_grad = lax.dot_general(
        recv_grads, down_weight, contract_last, preferred_element_type=jnp.float32
    )
    grad_gate_pre = (
        hidden_grad * up_pre * gate_sigmoid * (1.0 + gate_pre * (1.0 - gate_sigmoid))
    ).astype(jnp.bfloat16)
    grad_up_pre = (hidden_grad * gate_pre * gate_sigmoid).astype(jnp.bfloat16)
    down_total = lax.dot_general(
        hidden, recv_grads, contract_first, preferred_element_type=jnp.float32
    )
    gate_total = lax.dot_general(
        recv_tokens, grad_gate_pre, contract_first, preferred_element_type=jnp.float32
    )
    up_total = lax.dot_general(
        recv_tokens, grad_up_pre, contract_first, preferred_element_type=jnp.float32
    )
    row_part = (
        lax.dot_general(
            grad_gate_pre, gate_weight, contract_last, preferred_element_type=jnp.float32
        )
        + lax.dot_general(grad_up_pre, up_weight, contract_last, preferred_element_type=jnp.float32)
    ).astype(jnp.bfloat16)
    row_grad = share_sum(row_part).astype(jnp.bfloat16)
    back_grads = send_back(row_grad.reshape(expert_count, slot_count, slice_width)).reshape(
        local_rows, slice_width
    )
    slot_grads = lax.dot_general(
        placement, back_grads, contract_first, preferred_element_type=jnp.float32
    )
    token_grad = jnp.sum(slot_grads.reshape(token_count, top_count, slice_width), axis=1).astype(
        jnp.bfloat16
    )
    return (
        mixed,
        token_grad,
        route_grad,
        gate_total.astype(jnp.bfloat16)[None],
        up_total.astype(jnp.bfloat16)[None],
        down_total.astype(jnp.bfloat16)[None],
    )


def solution(mesh):
    in_specs = (
        P("expert", "dp"),
        P("expert", None),
        P("expert", None),
        P("expert", None, "dp"),
        P("expert", None, "dp"),
        P("expert", "dp", None),
        P("expert", "dp"),
    )
    out_specs = (
        P("expert", "dp"),
        P("expert", "dp"),
        P("expert", None),
        P("expert", None, "dp"),
        P("expert", None, "dp"),
        P("expert", "dp", None),
    )
    return jax.shard_map(shards, mesh=mesh, in_specs=in_specs, out_specs=out_specs, check_vma=False)
```

profile of v0, /device:TPU:0, one launch (start us, length us, event | category | flops | bytes accessed | tf_op | source)
XLA Modules:
  0.0 756.0 jit_solution(10491929963821267659)
XLA Ops:
  11.5 32.1 %all-gather.3.cloned.1.call-done = bf16[128,6144]{1,0:T(8,128)(2,1)} async-done(((bf16[128,1536]{1,0:T(8,128)(2,1)}), bf16[128,6144]{1,0:T(8,128)(2,1)}) %all-gather.3.cloned.1.call-update) | async-done | bytes 1572880 | tf_op jit(solution)/shard_map/all_gather | solution.py:11
  43.6 6.4 convolution_convert_fusion
  50.0 5.2 all-to-all-start
  56.2 33.1 %all-gather.5.cloned.1.call-done = bf16[128,6144]{1,0:T(8,128)(2,1)} async-done(((bf16[128,1536]{1,0:T(8,128)(2,1)}), bf16[128,6144]{1,0:T(8,128)(2,1)}) %all-gather.5.cloned.1.call-update) | async-done | bytes 1572880 | tf_op jit(solution)/shard_map/all_gather | solution.py:11
  89.2 7.7 %mul.87 = f32[128,4,6144]{2,1,0:T(4,128)} broadcast(bf16[128,6144]{1,0:T(8,128)(2,1)} %all-gather.5.cloned.1.call-done), dimensions={0,2} | broadcast | bytes 14155776 | tf_op jit(solution)/shard_map/mul | solution.py:74
  96.9 14.8 %mul.88 = f32[512,6144]{1,0:T(8,128)} reshape(f32[128,4,6144]{2,1,0:T(4,128)} %mul.87) | data formatting | bytes 25165824 | tf_op jit(solution)/shard_map/mul | solution.py:74
  111.7 12.2 %convolution_convert_fusion.1 = bf16[768,6144]{1,0:T(8,128)(2,1)} fusion(f32[512,6144]{1,0:T(8,128)} %mul.88, f32[512]{0:T(512)S(1)} %mul.85, s32[512]{0:T(512)S(1)} %multiply_add_fusion.1), kind=kOutput, calls=%fused_computation.3 | convolution fusion | flops 4843241472 | bytes 22024192 | tf_op jit(solution)/shard_map/dot_general | solution.py:77
  124.0 137.6 %all-to-all-done = bf16[8,96,6144]{2,1,0:T(8,128)(2,1)} async-done(((bf16[8,96,6144]{2,1,0:T(8,128)(2,1)}), bf16[8,96,6144]{2,1,0:T(8,128)(2,1)}, u32[]{:S(2)}, u32[]{:S(2)}) %all-to-all-start) | async-done | bytes 9437216 | tf_op jit(solution)/shard_map/all_to_all | solution.py:15
  261.5 5.2 all-to-all-start.2
  266.9 10.9 %fusion.7 = f32[768,512]{1,0:T(8,128)} fusion(bf16[768,6144]{1,0:T(8,128)(2,1)} %bitcast.3, bf16[1,6144,512]{2,1,0:T(8,128)(2,1)} %param.11), kind=kOutput, calls=%fused_computation.15 | convolution fusion | flops 4831838208 | bytes 17301504 | tf_op jit(solution)/shard_map/dot_general | solution.py:55
  277.8 8.7 %fusion.11 = f32[768,512]{1,0:T(8,128)} fusion(bf16[768,6144]{1,0:T(8,128)(2,1)} %bitcast.3, bf16[1,6144,512]{2,1,0:T(8,128)(2,1)S(1)} %bitcast.65), kind=kOutput, calls=%fused_computation.19 | convolution fusion | flops 4831838208 | bytes 17301504 | tf_op jit(solution)/shard_map/dot_general | solution.py:54
  286.6 186.5 %all-to-all-done.2 = bf16[8,96,6144]{2,1,0:T(8,128)(2,1)} async-done(((bf16[8,96,6144]{2,1,0:T(8,128)(2,1)}), bf16[8,96,6144]{2,1,0:T(8,128)(2,1)}, u32[]{:S(2)}, u32[]{:S(2)}) %all-to-all-start.2) | async-done | bytes 9437216 | tf_op jit(solution)/shard_map/all_to_all | solution.py:15
  473.1 11.1 %multiply_convert_fusion.2 = (bf16[768,512]{1,0:T(8,128)(2,1)S(1)}, bf16[768,512]{1,0:T(8,128)(2,1)S(1)}, bf16[768,512]{1,0:T(8,128)(2,1)S(1)}) fusion(f32[768,512]{1,0:T(8,128)} %fusion.11, f32[768,512]{1,0:T(8,128)} %fusion.7, bf16[768,6144]{1,0:T(8,128)(2,1)} %bitcast.11, bf16[1,512,6144]{2,1,0:T(8,128)(2,1)} %param.12), kind=kOutput, calls=%fused_computation.25 | convolution fusion | flops 4838129664 | bytes 21233664 | tf_op jit(solution)/shard_map/dot_general | solution.py:82
  484.2 11.0 %convolution_convert_fusion.2 = bf16[768,6144]{1,0:T(8,128)(2,1)} fusion(bf16[768,512]{1,0:T(8,128)(2,1)S(1)} %get-tuple-element.10, bf16[1,512,6144]{2,1,0:T(8,128)(2,1)} %param.12), kind=kOutput, calls=%fused_computation.4 | convolution fusion | flops 4836556800 | bytes 16515072 | tf_op jit(solution)/shard_map/dot_general | solution.py:58
  495.5 12.1 %fusion.9 = f32[768,6144]{1,0:T(8,128)} fusion(bf16[768,512]{1,0:T(8,128)(2,1)S(1)} %get-tuple-element.9, bf16[1,6144,512]{2,1,0:T(8,128)(2,1)} %param.10), kind=kOutput, calls=%fused_computation.17 | convolution fusion | flops 4831838208 | bytes 25952256 | tf_op jit(solution)/shard_map/dot_general | solution.py:99
  507.6 13.6 %add_convert_fusion = bf16[768,6144]{1,0:T(8,128)(2,1)} fusion(f32[768,6144]{1,0:T(8,128)} %fusion.9, bf16[768,512]{1,0:T(8,128)(2,1)S(1)} %get-tuple-element.8, bf16[1,6144,512]{2,1,0:T(8,128)(2,1)} %param.11), kind=kOutput, calls=%fused_computation | convolution fusion | flops 4841275392 | bytes 35389440 | tf_op jit(solution)/shard_map/dot_general | solution.py:102
  521.2 67.1 %reduce-scatter.3.cloned.1.call-done = bf16[768,1536]{1,0:T(8,128)(2,1)} async-done(((bf16[768,6144]{1,0:T(8,128)(2,1)}), bf16[768,1536]{1,0:T(8,128)(2,1)}) %reduce-scatter.3.cloned.1.call-update) | async-done | bytes 2359312 | tf_op jit(solution)/shard_map/reduce_scatter | solution.py:23
  588.2 4.6 all-to-all-start.1
  594.2 92.0 %reduce-scatter.5.cloned.1.call-done = bf16[768,1536]{1,0:T(8,128)(2,1)} async-done(((bf16[768,6144]{1,0:T(8,128)(2,1)}), bf16[768,1536]{1,0:T(8,128)(2,1)}) %reduce-scatter.5.cloned.1.call-update) | async-done | bytes 2359312 | tf_op jit(solution)/shard_map/reduce_scatter | solution.py:23
  690.8 10.9 %fusion = bf16[1,512,6144]{2,1,0:T(8,128)(2,1)} fusion(bf16[768,512]{1,0:T(8,128)(2,1)} %copy-done.7, bf16[768,6144]{1,0:T(8,128)(2,1)} %bitcast.11), kind=kOutput, calls=%fused_computation.8 | convolution fusion | flops 4834983936 | bytes 16515072 | tf_op jit(solution)/shard_map/dot_general | solution.py:89
  701.7 10.8 %fusion.2 = bf16[1,6144,512]{2,1,0:T(8,128)(2,1)} fusion(bf16[768,6144]{1,0:T(8,128)(2,1)} %bitcast.3, bf16[768,512]{1,0:T(8,128)(2,1)S(1)} %copy-done.4), kind=kOutput, calls=%fused_computation.10 | convolution fusion | flops 4834983936 | bytes 16515072 | tf_op jit(solution)/shard_map/dot_general | solution.py:95
  712.6 10.8 %fusion.1 = bf16[1,6144,512]{2,1,0:T(8,128)(2,1)} fusion(bf16[768,6144]{1,0:T(8,128)(2,1)} %bitcast.3, bf16[768,512]{1,0:T(8,128)(2,1)S(1)} %copy-done.6), kind=kOutput, calls=%fused_computation.9 | convolution fusion | flops 4834983936 | bytes 16515072 | tf_op jit(solution)/shard_map/dot_general | solution.py:92
  725.6 9.5 %psum.7 = f32[128,4]{0,1:T(4,128)} all-reduce(f32[128,4]{0,1:T(4,128)S(1)} %get-tuple-element.6), channel_id=1, replica_groups=mesh['dp'=4,'expert'=8] {'dp'}, use_global_device_ids=true, to_apply=%region_9.10 | all-reduce | flops 512 | bytes 4096 | tf_op jit(solution)/shard_map/psum | solution.py:72
  735.1 10.6 %all-to-all-done.3 = bf16[8,96,1536]{2,1,0:T(8,128)(2,1)} async-done(((bf16[8,96,1536]{2,1,0:T(8,128)(2,1)}), bf16[8,96,1536]{2,1,0:T(8,128)(2,1)}, u32[]{:S(2)}, u32[]{:S(2)}) %all-to-all-start.3) | async-done | bytes 2359328 | tf_op jit(solution)/shard_map/all_to_all | solution.py:19
  (52 shorter events, 17.9 us)
Async XLA Ops:
  7.2 36.4 %all-gather.3.cloned.1.call-start = ((), (), s32[]{:S(2)}) async-start(), calls=%async_computation.6 | async-start | bytes 1966080 | tf_op jit(solution)/shard_map/all_gather | solution.py:11
  50.0 5.9 copy-start.2
  50.0 211.5 %all-to-all-start = ((bf16[8,96,6144]{2,1,0:T(8,128)(2,1)}), bf16[8,96,6144]{2,1,0:T(8,128)(2,1)}, u32[]{:S(2)}, u32[]{:S(2)}) async-start(bf16[8,96,6144]{2,1,0:T(8,128)(2,1)} %bitcast.59), calls=%async_computation | async-start | bytes 18874368 | tf_op jit(solution)/shard_map/all_to_all | solution.py:15
  55.2 34.1 %all-gather.5.cloned.1.call-start = ((), (), s32[]{:S(2)}) async-start(), calls=%async_computation.8 | async-start | bytes 1966080 | tf_op jit(solution)/shard_map/all_gather | solution.py:11
  261.5 16.3 %slice-start = ((s8[6291456]{0:T(1024)(128)(4,1)}), s8[2097152]{0:T(1024)(128)(4,1)S(1)}, s32[]{:S(2)}) async-start(s8[6291456]{0:T(1024)(128)(4,1)} %bitcast.64), calls=%async_computation.10 | async-start | bytes 4194304
  261.5 211.5 %all-to-all-start.2 = ((bf16[8,96,6144]{2,1,0:T(8,128)(2,1)}), bf16[8,96,6144]{2,1,0:T(8,128)(2,1)}, u32[]{:S(2)}, u32[]{:S(2)}) async-start(bf16[8,96,6144]{2,1,0:T(8,128)(2,1)} %bitcast.60), calls=%async_computation.3 | async-start | bytes 18874368 | tf_op jit(solution)/shard_map/all_to_all | solution.py:15
  266.7 321.5 %reduce-scatter.3.cloned.1.call-start = ((), (), s32[]{:S(2)}) async-start(), calls=%async_computation.7 | async-start | bytes 11796480 | tf_op jit(solution)/shard_map/reduce_scatter | solution.py:23
  266.9 10.9 %slice-start.1 = ((s8[6291456]{0:T(1024)(128)(4,1)}), s8[4194304]{0:T(1024)(128)(4,1)S(1)}, s32[]{:S(2)}) async-start(s8[6291456]{0:T(1024)(128)(4,1)} %bitcast.64), calls=%async_computation.11 | async-start | bytes 8388608
  484.2 11.0 %copy-start.7 = (bf16[768,512]{1,0:T(8,128)(2,1)}, bf16[768,512]{1,0:T(8,128)(2,1)S(1)}, u32[]{:S(2)}) copy-start(bf16[768,512]{1,0:T(8,128)(2,1)S(1)} %get-tuple-element.10) | copy-start | bytes 2359300
  484.2 11.3 %copy-start.5 = (bf16[768,512]{1,0:T(8,128)(2,1)}, bf16[768,512]{1,0:T(8,128)(2,1)S(1)}, u32[]{:S(2)}) copy-start(bf16[768,512]{1,0:T(8,128)(2,1)S(1)} %get-tuple-element.9) | copy-start | bytes 2359300
  484.2 23.4 %copy-start.3 = (bf16[768,512]{1,0:T(8,128)(2,1)}, bf16[768,512]{1,0:T(8,128)(2,1)S(1)}, u32[]{:S(2)}) copy-start(bf16[768,512]{1,0:T(8,128)(2,1)S(1)} %get-tuple-element.8) | copy-start | bytes 2359300
  495.2 191.0 %reduce-scatter.5.cloned.1.call-start = ((), (), s32[]{:S(2)}) async-start(), calls=%async_computation.9 | async-start | bytes 11796480 | tf_op jit(solution)/shard_map/reduce_scatter | solution.py:23
  521.1 71.7 %copy-start = (bf16[128,1536]{1,0:T(8,128)(2,1)S(1)}, bf16[128,1536]{1,0:T(8,128)(2,1)}, u32[]{:S(2)}) copy-start(bf16[128,1536]{1,0:T(8,128)(2,1)} %param.13) | copy-start | bytes 1179652
  588.2 98.0 %all-to-all-start.1 = ((bf16[8,96,1536]{2,1,0:T(8,128)(2,1)}), bf16[8,96,1536]{2,1,0:T(8,128)(2,1)S(1)}, u32[]{:S(2)}, u32[]{:S(2)}) async-start(bf16[8,96,1536]{2,1,0:T(8,128)(2,1)} %bitcast.62), calls=%async_computation.2 | async-start | bytes 4718592 | tf_op jit(solution)/shard_map/all_to_all | solution.py:19
  686.2 59.4 %all-to-all-start.3 = ((bf16[8,96,1536]{2,1,0:T(8,128)(2,1)}), bf16[8,96,1536]{2,1,0:T(8,128)(2,1)}, u32[]{:S(2)}, u32[]{:S(2)}) async-start(bf16[8,96,1536]{2,1,0:T(8,128)(2,1)} %bitcast.61), calls=%async_computation.5 | async-start | bytes 4718592 | tf_op jit(solution)/shard_map/all_to_all | solution.py:19
  690.8 10.9 %copy-start.4 = (bf16[768,512]{1,0:T(8,128)(2,1)S(1)}, bf16[768,512]{1,0:T(8,128)(2,1)}, u32[]{:S(2)}) copy-start(bf16[768,512]{1,0:T(8,128)(2,1)} %copy-done.3) | copy-start | bytes 2359300
  701.7 10.9 %copy-start.6 = (bf16[768,512]{1,0:T(8,128)(2,1)S(1)}, bf16[768,512]{1,0:T(8,128)(2,1)}, u32[]{:S(2)}) copy-start(bf16[768,512]{1,0:T(8,128)(2,1)} %copy-done.5) | copy-start | bytes 2359300
  712.6 10.8 %copy-start.1 = (pred[128,4,768]{2,1,0:T(4,128)(4,1)S(1)}, pred[128,4,768]{2,1,0:T(4,128)(4,1)}, u32[]{:S(2)}) copy-start(pred[128,4,768]{2,1,0:T(4,128)(4,1)} %eq.71) | copy-start | bytes 1179652
Sparse Core Ops, SparseCore 0:
  9.8 33.6 all-gather.2
  57.9 31.3 all-gather.4
  495.3 92.8 reduce-scatter.2
  591.2 94.9 reduce-scatter.4
where the time goes:
time: 757 us; the launch traced here: 756 us
  waiting for transfers between devices  560 us (74%)
  matrix products  125 us (17%)
  local copies, waits for them, and re-layouts  25.1 us (3%)
  starting transfers between devices  20.1 us (3%)
  between operations  13.9 us (2%)
  blocking collectives  9.46 us (1%)
    all_to_all x2, waiting for transfers between devices, dispatch(): lax.all_to_all(blocks, 'expert', split_axis=0, concat_axis=0, tiled=True)  324 us
    reduce_scatter x2, waiting for transfers between devices, share_sum(): lax.psum_scatter(partial_value, 'dp', scatter_dimension=1, tiled=True)  159 us
    all_gather x2, waiting for transfers between devices, full_rows(): return lax.all_gather(block, 'dp', axis=1, tiled=True)  65.1 us
    mul x3, local copies, waits for them, and re-layouts, shards(): route_weights[:, :, None] * whole_grad[:, None, :].astype(jnp.float32)  22.6 us
  transfers between devices with their start and end apart: 8, of which 7 were waited for; matrix products, arithmetic and copies ran while one was open for 16% of the time, Pallas kernels for 0%

commit v1 on v0

v1 whole, which is shorter than its diff:
```python
import functools
import jax
import jax.numpy as jnp
from jax import lax
from jax.experimental import pallas as pl
from jax.experimental.pallas import tpu as pltpu
from jax.sharding import PartitionSpec as P

CORES = 2
contract_last = (((1,), (1,)), ((), ()))
contract_first = (((0,), (0,)), ((), ()))


def dot32(left, right, dims=(((1,), (0,)), ((), ()))):
    return lax.dot_general(left, right, dims, preferred_element_type=jnp.float32)


def line_groups(count):
    return [[i for i in range(count) if i % CORES == core] for core in range(CORES)]


def pair_groups(count):
    return [[i + core for core in range(CORES)] for i in range(0, count, CORES)]


def gather_rows(block):
    count = lax.axis_size("expert")
    line = lax.all_gather(block, "expert", axis=0, tiled=True, axis_index_groups=line_groups(count))
    wide = lax.all_gather(line, "dp", axis=1, tiled=True)
    return lax.all_gather(wide, "expert", axis=0, tiled=True, axis_index_groups=pair_groups(count))


def scatter_rows(partial_value):
    count = lax.axis_size("expert")
    half = lax.psum_scatter(
        partial_value, "expert", scatter_dimension=0, tiled=True, axis_index_groups=pair_groups(count)
    )
    narrow = lax.psum_scatter(half, "dp", scatter_dimension=1, tiled=True)
    return lax.psum_scatter(
        narrow, "expert", scatter_dimension=0, tiled=True, axis_index_groups=line_groups(count)
    )


def position():
    d = lax.axis_index("dp")
    e = lax.axis_index("expert")
    return d, e // CORES, e % CORES


def greet(d, z, c, chips, across, along):
    barrier = pltpu.get_barrier_semaphore()

    def signal(dd, zz, cc):
        pl.semaphore_signal(
            barrier, inc=1, device_id=(dd, zz * CORES + cc), device_id_type=pl.DeviceIdType.MESH
        )

    signal(across, z, c)
    signal(along, z, c)
    signal(d, z, 1 - c)
    pl.when(z > 0)(lambda: signal(d, z - 1, c))
    pl.when(z < chips - 1)(lambda: signal(d, z + 1, c))
    inner = jnp.where(z > 0, 1, 0) + jnp.where(z < chips - 1, 1, 0)
    pl.semaphore_wait(barrier, 3 + inner)


def gather_kernel(
    chips, t_in, g_in, w_in, t_out, g_out, w_out,
    own_sem, up_s, down_s, line_r, x_s, x_r, y_s, y_r, a_s, a_r, b_s, b_r, c_s, c_r,
):
    d, z, c = position()
    across = d + 1 - 2 * (d % 2)
    along = (d + 2) % 4
    diagonal = 3 - d
    columns = (d, across, along, diagonal)
    ins = (t_in, g_in, w_in)
    outs = (t_out, g_out, w_out)
    rows, width = t_in.shape

    def place(a, cc, zz, dd, half=None):
        slot = cc * chips + zz
        if a == 2:
            return outs[a].at[slot]
        first, size = slot * rows, rows
        if half is not None:
            size = rows // 2
            first = first + half * size
        return outs[a].at[
            pl.ds(pl.multiple_of(first, rows // 2), size), pl.ds(pl.multiple_of(dd * width, width), width)
        ]

    def send(src, dst, send_sem, recv_sem, dd, zz, cc):
        return pltpu.make_async_remote_copy(
            src_ref=src, dst_ref=dst, send_sem=send_sem, recv_sem=recv_sem,
            device_id=(dd, zz * CORES + cc), device_id_type=pl.DeviceIdType.MESH,
        )

    def source(a, zz, own):
        return ins[a] if own else place(a, c, zz, d)

    def up(a, zz, own=False):
        return send(source(a, zz, own), place(a, c, zz, d), up_s.at[a, zz], line_r.at[a, zz], d, z + 1, c)

    def down(a, zz, own=False):
        return send(source(a, zz, own), place(a, c, zz, d), down_s.at[a, zz], line_r.at[a, zz], d, z - 1, c)

    def go_x(a, zz, dd, own=False):
        src = ins[a] if own else place(a, c, zz, dd)
        return send(src, place(a, c, zz, dd), x_s.at[a, zz], x_r.at[a, zz], across, z, c)

    def go_y(a, zz, dd, own=False):
        src = ins[a] if own else place(a, c, zz, dd)
        return send(src, place(a, c, zz, dd), y_s.at[a, zz], y_r.at[a, zz], along, z, c)

    def go_a(a, zz, dd):
        part = place(a, c, zz, dd, 0)
        return send(part, part, a_s.at[a, zz], a_r.at[a, zz], along, z, c)

    def go_b(a, zz, dd):
        part = place(a, c, zz, dd, 1)
        return send(part, part, b_s.at[a, zz], b_r.at[a, zz], across, z, c)

    def pair(a, j, zz, cc, own=False):
        src = ins[a] if own else place(a, cc, zz, columns[j])
        return send(src, place(a, cc, zz, columns[j]), c_s.at[a, j, zz], c_r.at[a, j, zz], d, z, 1 - c)

    def spread(a, zz, own=False):
        if a < 2:
            go_x(a, zz, d, own).start()
            go_y(a, zz, d, own).start()
        pair(a, 0, zz, c, own).start()

    def line(a, distance):
        below, above = z - distance, z + distance

        @pl.when(below >= 0)
        def _():
            up(a, below).wait_recv()
            pl.when(z < chips - 1)(lambda: up(a, below).start())
            spread(a, below)

        @pl.when(above < chips)
        def _():
            down(a, above).wait_recv()
            pl.when(z > 0)(lambda: down(a, above).start())
            spread(a, above)

    def both(distance, act):
        for a in range(2):
            if distance == 0:
                act(a, z)
            else:
                pl.when(z - distance >= 0)(lambda: act(a, z - distance))
                pl.when(z + distance < chips)(lambda: act(a, z + distance))

    def plane(a, zz):
        go_x(a, zz, across).wait_recv()
        go_a(a, zz, across).start()
        pair(a, 1, zz, c).start()
        go_y(a, zz, along).wait_recv()
        go_b(a, zz, along).start()
        pair(a, 2, zz, c).start()

    def corner(a, zz):
        go_a(a, zz, diagonal).wait_recv()
        go_b(a, zz, diagonal).wait_recv()
        pair(a, 3, zz, c).start()

    greet(d, z, c, chips, across, along)
    for a in (2, 0, 1):
        pl.when(z < chips - 1)(lambda: up(a, z, True).start())
        pl.when(z > 0)(lambda: down(a, z, True).start())
        spread(a, z, True)
    locals_ = [pltpu.make_async_copy(ins[a], place(a, c, z, d), own_sem.at[a]) for a in range(3)]
    for copy in locals_:
        copy.start()
    for step in range(1, chips + 2):
        if step < chips:
            for a in (2, 0, 1):
                line(a, step)
        if step - 1 < chips:
            both(step - 1, plane)
        if 0 <= step - 2 < chips:
            both(step - 2, corner)
    for copy in locals_:
        copy.wait()
    for a in range(3):
        for zz in range(chips):
            for j in range(4 if a < 2 else 1):
                pair(a, j, zz, 1 - c).wait_recv()
                pair(a, j, zz, c).wait_send()
            if a < 2:
                go_x(a, zz, d).wait_send()
                go_y(a, zz, d).wait_send()
                go_a(a, zz, across).wait_send()
                go_b(a, zz, along).wait_send()
            pl.when((zz <= z) & (z < chips - 1))(lambda: up(a, zz).wait_send())
            pl.when((zz >= z) & (z > 0))(lambda: down(a, zz).wait_send())


def gather_all(tokens, grad_out, dense):
    count = lax.axis_size("expert")
    chips = count // CORES
    rows, width = tokens.shape
    whole = jax.ShapeDtypeStruct((count * rows, 4 * width), tokens.dtype)
    anywhere = pl.BlockSpec(memory_space=pl.ANY)
    dma = pltpu.SemaphoreType.DMA
    return pl.pallas_call(
        functools.partial(gather_kernel, chips),
        out_shape=(whole, whole, jax.ShapeDtypeStruct((count,) + dense.shape, dense.dtype)),
        in_specs=[anywhere] * 3,
        out_specs=(anywhere,) * 3,
        scratch_shapes=[dma((3,))]
        + [dma((3, chips))] * 3
        + [dma((2, chips))] * 8
        + [dma((3, 4, chips))] * 2,
        compiler_params=pltpu.CompilerParams(collective_id=0, has_side_effects=True),
        cost_estimate=pl.CostEstimate(flops=0, bytes_accessed=50_000_000, transcendentals=0),
    )(tokens, grad_out, dense)


def shards(tokens, expert_ids, route_weights, gate_weights, up_weights, down_weights, grad_out):
    count = lax.axis_size("expert")
    token_count = tokens.shape[0]
    me = lax.axis_index("expert")
    gate_weight = gate_weights[0]
    up_weight = up_weights[0]
    down_weight = down_weights[0]
    chosen = expert_ids[:, :, None] == jnp.arange(count, dtype=jnp.int32)
    dense = jnp.sum(jnp.where(chosen, route_weights[:, :, None], 0.0), axis=1)
    if lax.axis_size("dp") == 4 and count == 8:
        rows, grads, dense_all = gather_all(tokens, grad_out, dense.T)
        weight = lax.dynamic_index_in_dim(dense_all, me, axis=1, keepdims=False).reshape(-1, 1)
    else:
        dense_all = lax.all_gather(dense.T, "expert", axis=0)
        mine = lax.dynamic_index_in_dim(dense_all, me, axis=1, keepdims=False)
        weight = mine.reshape(count // CORES, CORES, token_count).transpose(1, 0, 2).reshape(-1, 1)
        rows = gather_rows(tokens)
        grads = gather_rows(grad_out)
    gate_pre = dot32(rows, gate_weight)
    up_pre = dot32(rows, up_weight)
    gate_sigmoid = jax.nn.sigmoid(gate_pre)
    hidden = gate_pre * gate_sigmoid * up_pre
    weighted = (weight * hidden).astype(jnp.bfloat16)
    mixed = scatter_rows(dot32(weighted, down_weight).astype(jnp.bfloat16))

    pulled = dot32(grads, down_weight, contract_last)
    route_part = jnp.sum(hidden * pulled, axis=1)
    hidden_grad = weight * pulled
    grad_gate_pre = (
        hidden_grad * up_pre * gate_sigmoid * (1.0 + gate_pre * (1.0 - gate_sigmoid))
    ).astype(jnp.bfloat16)
    grad_up_pre = (hidden_grad * gate_pre * gate_sigmoid).astype(jnp.bfloat16)
    row_part = (
        dot32(grad_gate_pre, gate_weight, contract_last)
        + dot32(grad_up_pre, up_weight, contract_last)
    ).astype(jnp.bfloat16)
    token_grad = scatter_rows(row_part)

    by_owner = route_part.reshape(CORES, count // CORES, token_count).transpose(1, 0, 2)
    own = lax.all_to_all(
        by_owner.reshape(count, token_count), "expert", split_axis=0, concat_axis=0, tiled=True
    )
    own = lax.psum(own, "dp")
    route_grad = jnp.sum(jnp.where(chosen, own.T[:, None, :], 0.0), axis=2)

    down_grad = dot32(weighted, grads, contract_first).astype(jnp.bfloat16)
    gate_grad = dot32(rows, grad_gate_pre, contract_first).astype(jnp.bfloat16)
    up_grad = dot32(rows, grad_up_pre, contract_first).astype(jnp.bfloat16)
    return (
        mixed,
        token_grad,
        route_grad,
        gate_grad[None],
        up_grad[None],
        down_grad[None],
    )


def solution(mesh):
    in_specs = (
        P("expert", "dp"),
        P("expert", None),
        P("expert", None),
        P("expert", None, "dp"),
        P("expert", None, "dp"),
        P("expert", "dp", None),
        P("expert", "dp"),
    )
    out_specs = (
        P("expert", "dp"),
        P("expert", "dp"),
        P("expert", None),
        P("expert", None, "dp"),
        P("expert", None, "dp"),
        P("expert", "dp", None),
    )
    return jax.shard_map(shards, mesh=mesh, in_specs=in_specs, out_specs=out_specs, check_vma=False)
```

time: 757 us -> 456 us (0.60)
  waiting for transfers between devices: 560 us -> 192 us
  Pallas kernels: 0 us -> 110 us
  local copies, waits for them, and re-layouts: 25.1 us -> 2.72 us
  starting transfers between devices: 20.1 us -> 5.24 us
    all_to_all x4 -> x1, waiting for transfers between devices: 335 us -> 0.01 us  [shards(): lax.all_to_all(by_owner.reshape(count, token_count), 'expert', split_axis...]
    pallas_call x0 -> x1, Pallas kernels: none -> 110 us  [gather_all(): pl.pallas_call(functools.partial(gather_kernel, chips), out_shape=(whole,...]
    all_gather x2 -> x0, waiting for transfers between devices: 65.1 us -> none  [full_rows(): return lax.all_gather(block, 'dp', axis=1, tiled=True)]
    reduce_scatter x2 -> x6, waiting for transfers between devices: 159 us -> 191 us  [the longest x2 130 us: scatter_rows(): narrow = lax.psum_scatter(half, 'dp', scatter_dimension=1, tiled=True)]
    mul x3 -> x0, local copies, waits for them, and re-layouts: 22.6 us -> none  [shards(): route_weights[:, :, None] * whole_grad[:, None, :].astype(jnp.float32)]
    all_to_all x4 -> x1, starting transfers between devices: 19.6 us -> 4.6 us  [shards(): lax.all_to_all(by_owner.reshape(count, token_count), 'expert', split_axis...]
    dot_general x13 -> x9, matrix products: 125 us -> 122 us  [dot32(): lax.dot_general(left, right, dims, preferred_element_type=jnp.float32)]
  transfers between devices with their start and end apart: 8 -> 7, of which waited for: 7 -> 5; matrix products, arithmetic and copies ran while one was open for 16% -> 19% of each run, Pallas kernels for 0% -> 0%
where the time goes in v1:
time: 456 us
  waiting for transfers between devices  192 us (42%)
  matrix products  122 us (27%)
  Pallas kernels  110 us (24%)
  between operations  14.2 us (3%)
  blocking collectives  8.84 us (2%)
  starting transfers between devices  5.24 us (1%)
    reduce_scatter x2, waiting for transfers between devices, scatter_rows(): narrow = lax.psum_scatter(half, 'dp', scatter_dimension=1, tiled=True)  130 us
    dot_general x9, matrix products, dot32(): lax.dot_general(left, right, dims, preferred_element_type=jnp.float32)  122 us
    pallas_call x1, Pallas kernels, gather_all(): pl.pallas_call(functools.partial(gather_kernel, chips), out_shape=(whole,...  110 us
    reduce_scatter x2, waiting for transfers between devices, scatter_rows(): lax.psum_scatter(narrow, 'expert', scatter_dimension=0, tiled=True, axis_...  40.3 us
    reduce_scatter x2, waiting for transfers between devices, scatter_rows(): lax.psum_scatter(partial_value, 'expert', scatter_dimension=0, tiled=True...  20.8 us
  transfers between devices with their start and end apart: 7, of which 5 were waited for; matrix products, arithmetic and copies ran while one was open for 19% of the time, Pallas kernels for 0%

profile of v1, /device:TPU:0, one launch (start us, length us, event | category | flops | bytes accessed | tf_op | source)
XLA Modules:
  0.0 456.0 jit_solution(16585965948122653343)
XLA Ops:
  7.2 1.3 select_reduce_fusion.1
  8.5 109.9 %shard_map.118 = (bf16[1024,6144]{1,0:T(8,128)(2,1)}, bf16[1024,6144]{1,0:T(8,128)(2,1)}, f32[8,8,128]{2,1,0:T(8,128)}) custom-call(bf16[128,1536]{1,0:T(8,128)(2,1)} %t_in.1, bf16[128,1536]{1,0:T(8,128)(2,1)} %g_in.1, f32[8,128]{1,0:T(8,128)} %bitcast.44), custom_call_target="tpu_custom_call" | custom-call | bytes 50000000 | tf_op jit(solution)/shard_map/pallas_call | solution.py:208
  118.5 12.6 %fusion.7 = f32[1024,512]{0,1:T(8,128)} fusion(bf16[1024,6144]{1,0:T(8,128)(2,1)} %get-tuple-element.10, bf16[1,6144,512]{2,1,0:T(8,128)(2,1)} %param.11), kind=kOutput, calls=%fused_computation.12 | convolution fusion | flops 6442450944 | bytes 20971520 | tf_op jit(solution)/shard_map/dot_general | solution.py:15
  131.2 10.9 %fusion.11 = f32[1024,512]{0,1:T(8,128)} fusion(bf16[1024,6144]{1,0:T(8,128)(2,1)} %get-tuple-element.10, bf16[1,6144,512]{2,1,0:T(8,128)(2,1)S(1)} %bitcast.51), kind=kOutput, calls=%fused_computation.16 | convolution fusion | flops 6442450944 | bytes 20971520 | tf_op jit(solution)/shard_map/dot_general | solution.py:15
  142.1 0.8 constant_dynamic-slice_fusion
  142.8 13.0 %convolution_convert_fusion = bf16[1024,6144]{1,0:T(8,128)(2,1)} fusion(bf16[1,512,6144]{2,1,0:T(8,128)(2,1)} %param.12, f32[1024]{0:T(1024)S(1)} %bitcast.46, f32[1024,512]{0,1:T(8,128)} %fusion.7, f32[1024,512]{0,1:T(8,128)} %fusion.11), kind=kOutput, calls=%fused_computation.1 | convolution fusion | flops 6452412416 | bytes 23072768 | tf_op jit(solution)/shard_map/dot_general | solution.py:15
  156.0 1.3 copy-done.1
  157.4 14.7 %multiply_reduce_fusion = (f32[1024]{0:T(1024)S(1)}, bf16[1024,512]{0,1:T(8,128)(2,1)S(1)}, bf16[1024,512]{0,1:T(8,128)(2,1)S(1)}) fusion(f32[1024,512]{0,1:T(8,128)S(1)} %copy-done.1, f32[1024,512]{0,1:T(8,128)} %fusion.11, f32[1024]{0:T(1024)S(1)} %bitcast.47, bf16[1024,6144]{1,0:T(8,128)(2,1)} %get-tuple-element.11, bf16[1,512,6144]{2,1,0:T(8,128)(2,1)} %param.12), kind=kOutput, calls=%fused_computation.18 | convolution fusion | flops 6451887104 | bytes 25174016 | tf_op jit(solution)/shard_map/dot_general | solution.py:15
  172.1 15.9 %fusion.9 = f32[1024,6144]{1,0:T(8,128)} fusion(bf16[1024,512]{0,1:T(8,128)(2,1)S(1)} %get-tuple-element.13, bf16[1,6144,512]{2,1,0:T(8,128)(2,1)} %param.10), kind=kOutput, calls=%fused_computation.14 | convolution fusion | flops 6442450944 | bytes 32505856 | tf_op jit(solution)/shard_map/dot_general | solution.py:15
  188.0 16.9 %add_convert_fusion = bf16[1024,6144]{1,0:T(8,128)(2,1)} fusion(f32[1024,6144]{1,0:T(8,128)} %fusion.9, bf16[1024,512]{0,1:T(8,128)(2,1)S(1)} %get-tuple-element.14, bf16[1,6144,512]{2,1,0:T(8,128)(2,1)} %param.11), kind=kOutput, calls=%fused_computation | convolution fusion | flops 6455033856 | bytes 45088768 | tf_op jit(solution)/shard_map/dot_general | solution.py:15
  205.0 0.7 reduce-scatter.9.cloned.1.call-update
  205.8 20.8 %reduce-scatter.13.cloned.1.call-done = bf16[512,6144]{1,0:T(8,128)(2,1)} async-done(((bf16[1024,6144]{1,0:T(8,128)(2,1)}), bf16[512,6144]{1,0:T(8,128)(2,1)}) %reduce-scatter.13.cloned.1.call-update) | async-done | bytes 6291472 | tf_op jit(solution)/shard_map/reduce_scatter | solution.py:35
  226.7 74.3 %reduce-scatter.9.cloned.1.call-done = bf16[512,1536]{1,0:T(8,128)(2,1)} async-done(((bf16[512,6144]{1,0:T(8,128)(2,1)}), bf16[512,1536]{1,0:T(8,128)(2,1)}) %reduce-scatter.9.cloned.1.call-update) | async-done | bytes 1572880 | tf_op jit(solution)/shard_map/reduce_scatter | solution.py:38
  301.0 0.6 copy.24
  301.6 4.6 %all-to-all-start = ((f32[8,1,128]{2,1,0:T(1,128)}), f32[8,1,128]{2,1,0:T(1,128)S(1)}, u32[]{:S(2)}, u32[]{:S(2)}) async-start(f32[8,1,128]{2,1,0:T(1,128)} %bitcast.8), calls=%async_computation.6 | async-start | bytes 8192 | tf_op jit(solution)/shard_map/all_to_all | solution.py:261
  306.2 0.3 reduce-scatter.17.cloned.1.call-start
  306.5 12.2 %fusion = bf16[1,512,6144]{2,1,0:T(8,128)(2,1)} fusion(bf16[1024,6144]{1,0:T(8,128)(2,1)} %get-tuple-element.11, f32[1024]{0:T(1024)S(1)} %bitcast.48, f32[1024,512]{0,1:T(8,128)S(1)} %copy-done.1, f32[1024,512]{0,1:T(8,128)} %fusion.11), kind=kOutput, calls=%fused_computation.5 | convolution fusion | flops 6449266688 | bytes 23072768 | tf_op jit(solution)/shard_map/dot_general | solution.py:15
  318.7 55.4 %reduce-scatter.15.cloned.1.call-done = bf16[512,1536]{1,0:T(8,128)(2,1)} async-done(((bf16[512,6144]{1,0:T(8,128)(2,1)}), bf16[512,1536]{1,0:T(8,128)(2,1)}) %reduce-scatter.15.cloned.1.call-update) | async-done | bytes 1572880 | tf_op jit(solution)/shard_map/reduce_scatter | solution.py:38
  374.1 11.7 %fusion.1 = bf16[1,6144,512]{2,1,0:T(8,128)(2,1)} fusion(bf16[1024,6144]{1,0:T(8,128)(2,1)} %get-tuple-element.10, bf16[1024,512]{0,1:T(8,128)(2,1)} %copy-done.2), kind=kOutput, calls=%fused_computation.6 | convolution fusion | flops 6445596672 | bytes 19922944 | tf_op jit(solution)/shard_map/dot_general | solution.py:15
  385.8 13.6 %fusion.2 = bf16[1,6144,512]{2,1,0:T(8,128)(2,1)} fusion(bf16[1024,6144]{1,0:T(8,128)(2,1)} %get-tuple-element.10, bf16[1024,512]{0,1:T(8,128)(2,1)S(1)} %get-tuple-element.14), kind=kOutput, calls=%fused_computation.7 | convolution fusion | flops 6445596672 | bytes 19922944 | tf_op jit(solution)/shard_map/dot_general | solution.py:15
  399.4 8.8 %psum.7 = f32[128,8]{0,1:T(8,128)S(1)} all-reduce(f32[128,8]{0,1:T(8,128)S(1)} %bitcast.45), channel_id=1, replica_groups=mesh['dp'=4,'expert'=8] {'dp'}, use_global_device_ids=true, to_apply=%region_8.9 | all-reduce | flops 1024 | bytes 8192 | tf_op jit(solution)/shard_map/psum | solution.py:264
  408.3 0.6 select_reduce_fusion
  408.9 3.2 reduce-scatter.11.cloned.1.call-done
  412.1 37.0 %reduce-scatter.17.cloned.1.call-done = bf16[128,1536]{1,0:T(8,128)(2,1)} async-done(((bf16[512,1536]{1,0:T(8,128)(2,1)}), bf16[128,1536]{1,0:T(8,128)(2,1)}) %reduce-scatter.17.cloned.1.call-update) | async-done | bytes 393232 | tf_op jit(solution)/shard_map/reduce_scatter | solution.py:39
  (22 shorter events, 0.5 us)
Async XLA Ops:
  7.2 197.9 %reduce-scatter.7.cloned.1.call-start = ((), (), s32[]{:S(2)}) async-start(), calls=%async_computation.7 | async-start | bytes 18874368 | tf_op jit(solution)/shard_map/reduce_scatter | solution.py:35
  8.5 122.6 %slice-start = ((s8[6291456]{0:T(1024)(128)(4,1)}), s8[2097152]{0:T(1024)(128)(4,1)S(1)}, s32[]{:S(2)}) async-start(s8[6291456]{0:T(1024)(128)(4,1)} %bitcast.50), calls=%async_computation.13 | async-start | bytes 4194304
  118.5 12.7 %slice-start.1 = ((s8[6291456]{0:T(1024)(128)(4,1)}), s8[4194304]{0:T(1024)(128)(4,1)S(1)}, s32[]{:S(2)}) async-start(s8[6291456]{0:T(1024)(128)(4,1)} %bitcast.50), calls=%async_computation.14 | async-start | bytes 8388608
  155.8 1.6 copy-start.1
  155.8 70.8 %reduce-scatter.13.cloned.1.call-start = ((), (), s32[]{:S(2)}) async-start(), calls=%async_computation.10 | async-start | bytes 18874368 | tf_op jit(solution)/shard_map/reduce_scatter | solution.py:35
  172.1 15.9 %copy-start.2 = (bf16[1024,512]{0,1:T(8,128)(2,1)}, bf16[1024,512]{0,1:T(8,128)(2,1)S(1)}, u32[]{:S(2)}) copy-start(bf16[1024,512]{0,1:T(8,128)(2,1)S(1)} %get-tuple-element.13) | copy-start | bytes 3145732
  205.0 96.0 %reduce-scatter.9.cloned.1.call-start = ((), (), s32[]{:S(2)}) async-start(), calls=%async_computation.8 | async-start | bytes 7864320 | tf_op jit(solution)/shard_map/reduce_scatter | solution.py:38
  205.7 168.4 %reduce-scatter.15.cloned.1.call-start = ((), (), s32[]{:S(2)}) async-start(), calls=%async_computation.11 | async-start | bytes 7864320 | tf_op jit(solution)/shard_map/reduce_scatter | solution.py:38
  226.6 185.5 %reduce-scatter.11.cloned.1.call-start = ((), (), s32[]{:S(2)}) async-start(), calls=%async_computation.9 | async-start | bytes 1966080 | tf_op jit(solution)/shard_map/reduce_scatter | solution.py:39
  301.6 97.8 %all-to-all-start = ((f32[8,1,128]{2,1,0:T(1,128)}), f32[8,1,128]{2,1,0:T(1,128)S(1)}, u32[]{:S(2)}, u32[]{:S(2)}) async-start(f32[8,1,128]{2,1,0:T(1,128)} %bitcast.8), calls=%async_computation.6 | async-start | bytes 8192 | tf_op jit(solution)/shard_map/all_to_all | solution.py:261
  306.2 142.9 %reduce-scatter.17.cloned.1.call-start = ((), (), s32[]{:S(2)}) async-start(), calls=%async_computation.12 | async-start | bytes 1966080 | tf_op jit(solution)/shard_map/reduce_scatter | solution.py:39
  385.8 22.4 %copy-start = (s32[128,4]{0,1:T(4,128)S(1)}, s32[128,4]{0,1:T(4,128)}, u32[]{:S(2)}) copy-start(s32[128,4]{0,1:T(4,128)} %param.8) | copy-start | bytes 6148
Sparse Core Ops, SparseCore 0:
  155.9 21.7 reduce-scatter.6
  205.1 21.4 reduce-scatter.12
  229.6 71.3 reduce-scatter.8
  303.8 70.2 reduce-scatter.14
  376.8 35.2 reduce-scatter.10
  414.8 34.2 reduce-scatter.16
